TPU v7x, 256 devices: a whole 4x4x8 slice. The times are simulated.
256 devices in a mesh: ens: 16 (over z_lo, y), grid: 16 (over x, z_hi, core).
Axes of the slice: x: 4, y: 4, z: 8 (z_hi: 2, z_lo: 4; z = z_hi * 4 + z_lo), core: 2. Of those that a mesh axis runs over, the one named last changes fastest.
Arguments:
- entry_latent_embedding: bfloat16 [16, 4096, 1024], P('ens', 'grid'), may hold values from -16 to 16
- q_weight: bfloat16 [1024, 1024], replicated, may hold values from -1 to 1, as said below
- k_weight: bfloat16 [1024, 1024], replicated, may hold values from -1 to 1, as said below
- v_weight: bfloat16 [1024, 1024], replicated, may hold values from -0.1875 to 0.1875
- o_weight: bfloat16 [1024, 1024], replicated, may hold values from -0.1875 to 0.1875
- channel_to_field_map: bfloat16 [100, 1024], replicated, may hold values from -0.1875 to 0.1875
- targets: float32 [100, 4096], P(None, 'grid'), may hold values from -6 to 6
- area_weight: float32 [4096], P('grid'), may hold values from 0.4 to 4.8
- key_blocks: int32 [32, 3], P('grid'), may hold values from 0 to 31, as said below
Outputs:
- grad_hidden: bfloat16 [16, 4096, 1024], P('ens', 'grid')
- mean_loss: float32 [], replicated
Inputs may be any that keep to these rules, and one draw needn't show every extreme that they name: `key_blocks`: row b starts with b itself, then 3 - 1 further distinct blocks no more than 2 away from b and inside the grid. `q_weight`: projection scaled by its fan-in. `k_weight`: projection scaled by its fan-in.
All inputs are finite; a program needn't handle non-finite values.
Results may differ from a plain program's by a relative error of at most 0.025.
The roundings to bfloat16 on the way count: a program that leaves them out, or rounds other values in their place, can miss the bound.
Values may be sent and summed in bfloat16 or wider, within the bound.
A program may use at most 128 MiB of HBM per device.

v0:
```python
import functools

import jax
import jax.numpy as jnp
from jax import lax
from jax.experimental import pallas as pl
from jax.experimental.pallas import tpu as pltpu
from jax.sharding import PartitionSpec as P

MESH = pl.DeviceIdType.MESH
SMOOTH = 0.25
BIG = 1e30
NEG = -1e30
F32 = jnp.float32
BF16 = jnp.bfloat16


def nt(a, b):
    return lax.dot_general(a, b, (((1,), (1,)), ((), ())), preferred_element_type=F32)


def nn(a, b):
    return lax.dot_general(a, b, (((1,), (0,)), ((), ())), preferred_element_type=F32)


def heads_of(row):
    return jnp.concatenate(
        [
            jnp.broadcast_to(row[:, :128], (64, 128)),
            jnp.broadcast_to(row[:, 128:], (64, 128)),
        ],
        axis=0,
    )


def diagonal(pair):
    return jnp.concatenate([pair[:64, :128], pair[64:, 128:]], axis=0)


def kernel(
    ne,
    ng,
    kb_ref,
    x_hbm,
    wq_hbm,
    wk_hbm,
    wv_hbm,
    wo_hbm,
    mp_hbm,
    truth_ref,
    weight_ref,
    out_ref,
    loss_ref,
    WQ,
    WK,
    WV,
    WO,
    MP,
    X,
    K,
    V,
    KT,
    VT,
    QQ,
    DD,
    E,
    ACC,
    MS,
    L,
    LSE,
    LO,
    LR,
    MIXF,
    MIXB,
    OUTB,
    FC,
    RV,
    Y,
    G,
    GF,
    PF,
    DO,
    DOB,
    DQ,
    DK,
    DV,
    DKB,
    DVB,
    C,
    CR,
    LS,
    loc,
    xs,
    xr,
    a1s,
    a1r,
    a2s,
    a2r,
    gs,
    gr,
    ls,
    lr,
    cs,
    cr,
    ts,
    tr,
):
    e = lax.axis_index("ens")
    g = lax.axis_index("grid")
    core = lax.rem(g, 2)
    far = g - 1 + 2 * core
    near = g + 1 - 2 * core
    has_far = (far >= 0) & (far < ng)

    def load(src, dst, i):
        return pltpu.make_async_copy(src, dst, loc.at[i])

    lx = [
        load(x_hbm.at[pl.ds(pl.multiple_of(core * 128, 128), 128)], X.at[2], 0),
        load(x_hbm.at[pl.ds(pl.multiple_of((1 - core) * 128, 128), 128)], X.at[3], 1),
    ]
    lk, lv, lq = load(wk_hbm, WK, 2), load(wv_hbm, WV, 3), load(wq_hbm, WQ, 4)
    lo, lm = load(wo_hbm, WO, 5), load(mp_hbm, MP, 6)
    for c in lx + [lk, lv, lq, lo, lm]:
        c.start()

    barrier = pltpu.get_barrier_semaphore()

    @pl.loop(1, ne)
    def _(d):
        pl.semaphore_signal(barrier, inc=1, device_id=(lax.rem(e + d, ne), g), device_id_type=MESH)

    @pl.loop(1, ng)
    def _(d):
        pl.semaphore_signal(barrier, inc=1, device_id=(e, lax.rem(g + d, ng)), device_id_type=MESH)

    @pl.when(jnp.logical_not(has_far))
    def _():
        X[0:2] = jnp.zeros((2, 128, 1024), BF16)
        GF[0:2] = jnp.zeros((2, 128, 128), BF16)
        LR[0] = jnp.full((3, 8, 256), BIG, F32)
        CR[0] = jnp.zeros((2, 8, 256), F32)

    for c in lx:
        c.wait()
    pl.semaphore_wait(barrier, ne - 1 + ng - 1)

    def to(src, dst, s, r, dev):
        return pltpu.make_async_remote_copy(
            src_ref=src, dst_ref=dst, send_sem=s, recv_sem=r, device_id=dev, device_id_type=MESH
        )

    x_far = [to(X.at[2], X.at[1], xs.at[0], xr.at[0], (e, far)), to(X.at[3], X.at[0], xs.at[1], xr.at[1], (e, far))]
    x_near = [to(X.at[3], X.at[4], xs.at[2], xr.at[2], (e, near)), to(X.at[2], X.at[5], xs.at[3], xr.at[3], (e, near))]

    @pl.when(has_far)
    def _():
        for c in x_far:
            c.start()

    for c in x_near:
        c.start()

    def slot_of(block):
        return jnp.where(core == 0, block - (2 * g - 2), 2 * g + 3 - block)

    seen = []
    for q in range(2):
        ids = [jnp.where(core == 0, slot_of(kb_ref[q, n]), slot_of(kb_ref[1 - q, n])) for n in range(3)]
        seen.append([(ids[0] == s) | (ids[1] == s) | (ids[2] == s) for s in range(6)])

    low = lax.broadcasted_iota(jnp.int32, (1, 128), 1) < 64

    def stacked(block):
        zero = jnp.zeros_like(block)
        return jnp.concatenate([jnp.where(low, block, zero), jnp.where(low, zero, block)], axis=0)

    def rows_of(ref, slot, count):
        return ref[slot : slot + count].reshape(count * 128, 1024)

    def project_kv(W, D, DT, slot, count):
        @pl.loop(0, 4)
        def _(j):
            r = nn(rows_of(X, slot, count), W[:, pl.ds(pl.multiple_of(j * 256, 256), 256)]).astype(BF16)
            for h in range(2):
                part = r[:, h * 128 : (h + 1) * 128]
                D[2 * j + h, slot * 128 : (slot + count) * 128, :] = part
                DT[2 * j + h, :, slot * 128 : (slot + count) * 128] = part.T

    def project_q(slot, count):
        @pl.loop(0, 4)
        def _(j):
            r = nn(rows_of(X, slot, count), WQ[:, pl.ds(pl.multiple_of(j * 256, 256), 256)]).astype(BF16)
            r = (r.astype(F32) * 0.125).astype(BF16)
            for h in range(2):
                for i in range(count):
                    QQ[2 * j + h, slot + i] = stacked(r[i * 128 : (i + 1) * 128, h * 128 : (h + 1) * 128])

    def attend(qi, first, last, step, final):
        n = last - first + 1
        off = (first - qi) * 128

        @pl.loop(0, 8)
        def _(hp):
            row = pl.ds(hp, 1)
            s = nt(K[hp, first * 128 : (last + 1) * 128, :], QQ[hp, 2 + qi])
            if step:
                m_old = MS[qi, step - 1, row, :]
                m = m_old
            else:
                m = jnp.full((1, 256), NEG, F32)
            parts = [s[i * 128 : (i + 1) * 128] for i in range(n)]
            for i, part in enumerate(parts):
                m = jnp.maximum(m, jnp.where(seen[qi][first + i], jnp.max(part, axis=0, keepdims=True), NEG))
            total = jnp.zeros((1, 256), F32)
            exps = []
            for i, part in enumerate(parts):
                x = jnp.exp(part - jnp.where(seen[qi][first + i], m, BIG))
                total = total + jnp.sum(x, axis=0, keepdims=True)
                exps.append(x.astype(BF16))
            eb = jnp.concatenate(exps, axis=0) if n > 1 else exps[0]
            E[qi, hp, off : off + n * 128, :] = eb
            acc = diagonal(nn(VT[hp, :, first * 128 : (last + 1) * 128], eb))
            if step:
                alpha = jnp.exp(m_old - m)
                total = total + L[qi, row, :] * alpha
                acc = acc + ACC[qi, hp] * heads_of(alpha)
            MS[qi, step, row, :] = m
            if final:
                LSE[qi, row, :] = m + jnp.log(total)
                mix = (acc * heads_of(1.0 / total)).T
                lanes = pl.ds(pl.multiple_of(hp * 128, 128), 128)
                MIXF[qi, :, lanes] = mix
                MIXB[qi, :, lanes] = mix.astype(BF16)
            else:
                L[qi, row, :] = total
                ACC[qi, hp] = acc

    def decode(qi):
        @pl.loop(0, 4)
        def _(j):
            lanes = pl.ds(pl.multiple_of(j * 256, 256), 256)
            r = X[2 + qi, :, lanes].astype(F32) + nn(MIXB[qi], WO[:, lanes])
            OUTB[qi, :, lanes] = r.astype(BF16)

        FC[qi] = nt(OUTB[qi], MP[...]).astype(BF16)

    def place(t):
        half = t // 8
        return jnp.where(core == 0, half, 1 - half), pl.multiple_of(lax.rem(t, 8) * 16, 16)

    def a1(d):
        t = lax.rem(e + d, ne)
        b, r = place(t)
        return to(FC.at[b, pl.ds(r, 16)], RV.at[e], a1s.at[d], a1r.at[d], (t, g))

    lk.wait()
    lv.wait()
    project_kv(WK, K, KT, 2, 2)
    project_kv(WV, V, VT, 2, 2)
    lq.wait()
    project_q(2, 2)
    for c in x_near:
        c.wait_recv()
    project_kv(WK, K, KT, 4, 2)
    project_kv(WV, V, VT, 4, 2)
    attend(0, 2, 4, 0, False)
    attend(1, 2, 5, 0, False)
    project_q(4, 2)
    lo.wait()
    lm.wait()

    @pl.when(has_far)
    def _():
        x_far[0].wait_recv()

    project_kv(WK, K, KT, 1, 1)
    project_kv(WV, V, VT, 1, 1)
    attend(1, 1, 1, 1, True)
    attend(0, 1, 1, 1, False)
    decode(1)

    @pl.when(has_far)
    def _():
        x_far[1].wait_recv()

    project_kv(WK, K, KT, 0, 1)
    project_kv(WV, V, VT, 0, 1)
    attend(0, 0, 0, 2, True)
    decode(0)

    @pl.loop(1, ne)
    def _(d):
        a1(d).start()

    b_own, r_own = place(e)
    RV[e] = FC[b_own, pl.ds(r_own, 16), :]

    def shown(qi, s):
        return jnp.where(seen[qi][s], LSE[qi], BIG)

    LO[0, 0], LO[0, 1], LO[0, 2] = shown(0, 1), shown(0, 0), shown(1, 1)
    LO[1, 0], LO[1, 1], LO[1, 2] = shown(1, 5), shown(1, 4), shown(0, 4)
    l_far = to(LO.at[0], LR.at[0], ls.at[0], lr.at[0], (e, far))
    l_near = to(LO.at[1], LR.at[1], ls.at[1], lr.at[1], (e, near))

    @pl.when(has_far)
    def _():
        l_far.start()

    l_near.start()

    @pl.loop(0, 8)
    def _(hp):
        row = pl.ds(hp, 1)
        for qi in range(2):
            lse = LSE[qi, row, :]
            spans = ((2, 4), (1, 1), (0, 0)) if qi == 0 else ((2, 5), (1, 1))
            for step, (first, last) in enumerate(spans):
                scale = jnp.exp(MS[qi, step, row, :] - lse)
                a, b = (first - qi) * 128, (last + 1 - qi) * 128
                E[qi, hp, a:b, :] = (E[qi, hp, a:b, :].astype(F32) * scale).astype(BF16)

    project_q(0, 2)

    sides = ((1, 0, 256), (4, 5, 384))

    def foreign(side):
        q1, q2, k2 = sides[side]

        @pl.loop(0, 8)
        def _(hp):
            row = pl.ds(hp, 1)
            s1 = nt(K[hp, 256:512, :], QQ[hp, q1])
            PF[side, hp, 0:128] = jnp.exp(s1[:128] - LR[side, 0, row, :]).astype(BF16)
            PF[side, hp, 128:256] = jnp.exp(s1[128:] - LR[side, 1, row, :]).astype(BF16)
            s2 = nt(K[hp, k2 : k2 + 128, :], QQ[hp, q2])
            PF[side, hp, 256:384] = jnp.exp(s2 - LR[side, 2, row, :]).astype(BF16)

    l_near.wait_recv()
    foreign(1)

    @pl.loop(1, ne)
    def _(d):
        a1(d).wait_recv()

    Y[...] = RV[...].astype(F32)
    truth = truth_ref[...]
    weight = weight_ref[...]

    def score(i, total):
        y = Y[i]
        d = y - truth
        v = d * d + SMOOTH * SMOOTH
        r = lax.rsqrt(v)
        pd = y[None] - Y[...]
        pv = pd * pd + SMOOTH * SMOOTH
        pr = lax.rsqrt(pv)
        grad = weight * (d * r - jnp.sum(pd * pr, axis=0) / (ne - 1))
        G[i] = grad.astype(BF16)
        return total + (v * r - jnp.sum(pv * pr, axis=0) / (2.0 * (ne - 1)))

    total = lax.fori_loop(0, ne, score, jnp.zeros((16, 128), F32))
    partial = jnp.sum(jnp.sum(total * weight, axis=0, keepdims=True), axis=1, keepdims=True)
    p_hi = partial.astype(BF16).astype(F32)
    p_mid = (partial - p_hi).astype(BF16).astype(F32)
    p_lo = partial - p_hi - p_mid
    lane = lax.broadcasted_iota(jnp.int32, (16, 128), 1)
    first_row = lax.broadcasted_iota(jnp.int32, (16, 128), 0) == 0
    rider = jnp.where(lane == 104, p_hi, jnp.where(lane == 105, p_mid, jnp.where(lane == 106, p_lo, 0.0)))
    rider = jnp.where(first_row, rider, 0.0)

    def ride(i, carry):
        G[i] = (G[i].astype(F32) + rider).astype(BF16)
        return carry

    lax.fori_loop(0, ne, ride, 0)

    def a2(d):
        t = lax.rem(e + d, ne)
        b, r = place(e)
        return to(G.at[t], GF.at[2 + b, pl.ds(r, 16)], a2s.at[d], a2r.at[d], (t, g))

    @pl.loop(1, ne)
    def _(d):
        a2(d).start()

    GF[2 + b_own, pl.ds(r_own, 16), :] = G[e]

    @pl.when(has_far)
    def _():
        l_far.wait_recv()

    foreign(0)

    def a2_in(d):
        b, r = place(lax.rem(e - d + ne, ne))
        return to(G.at[0], GF.at[2 + b, pl.ds(r, 16)], a2s.at[d], a2r.at[d], (e, g))

    @pl.loop(1, ne)
    def _(d):
        a2_in(d).wait_recv()

    g_far = [to(GF.at[2], GF.at[1], gs.at[0], gr.at[0], (e, far)), to(GF.at[3], GF.at[0], gs.at[1], gr.at[1], (e, far))]
    g_near = [to(GF.at[3], GF.at[4], gs.at[2], gr.at[2], (e, near)), to(GF.at[2], GF.at[5], gs.at[3], gr.at[3], (e, near))]

    @pl.when(has_far)
    def _():
        for c in g_far:
            c.start()

    for c in g_near:
        c.start()

    mine = GF[2:4].reshape(256, 128).astype(F32)
    lane = lax.broadcasted_iota(jnp.int32, (256, 128), 1)
    mine = jnp.where((lane >= 104) & (lane < 107), mine, 0.0)
    band = jnp.sum(jnp.sum(mine, axis=0, keepdims=True), axis=1, keepdims=True)
    LS[g] = jnp.broadcast_to(band, (8, 128))

    def tell(d):
        return to(LS.at[g], LS.at[g], ts.at[d], tr.at[d], (e, lax.rem(g + d, ng)))

    def told(d):
        s = lax.rem(g - d + ng, ng)
        return to(LS.at[s], LS.at[s], ts.at[d], tr.at[d], (e, g))

    @pl.loop(1, ng)
    def _(d):
        tell(d).start()

    indicator = (lax.broadcasted_iota(jnp.int32, (8, 128), 1) // 64) == lax.broadcasted_iota(jnp.int32, (8, 128), 0)
    indicator = jnp.where(indicator, 1.0, 0.0).astype(BF16)

    def d_mix(slot, count, own):
        @pl.loop(0, 4)
        def _(j):
            lanes = pl.ds(pl.multiple_of(j * 256, 256), 256)
            r = nn(GF[slot : slot + count].reshape(count * 128, 128), MP[:, lanes])
            if own:
                DO[:, lanes] = r
            DOB[slot * 128 : (slot + count) * 128, lanes] = r.astype(BF16)

        @pl.loop(0, 4)
        def _(j):
            lanes = pl.ds(pl.multiple_of(j * 256, 256), 256)
            r = nt(DOB[slot * 128 : (slot + count) * 128, :], WO[lanes, :]).astype(BF16)
            for h in range(2):
                for i in range(count):
                    part = r[i * 128 : (i + 1) * 128, h * 128 : (h + 1) * 128]
                    DD[2 * j + h, slot + i] = stacked(part)
                    if own:
                        hp_lanes = pl.ds(pl.multiple_of(j * 256 + h * 128, 128), 128)
                        prod = part.astype(F32) * MIXF[i, :, hp_lanes]
                        hi = prod.astype(BF16)
                        low_part = (prod - hi.astype(F32)).astype(BF16)
                        c = nt(indicator, hi) + nt(indicator, low_part)
                        C[i, pl.ds(2 * j + h, 1), :] = jnp.concatenate([c[0:1], c[1:2]], axis=1)

    d_mix(2, 2, True)
    c_far = to(C, CR.at[0], cs.at[0], cr.at[0], (e, far))
    c_near = to(C, CR.at[1], cs.at[1], cr.at[1], (e, near))

    @pl.when(has_far)
    def _():
        c_far.start()

    c_near.start()

    @pl.loop(0, 8)
    def _(hp):
        row = pl.ds(hp, 1)
        dk = jnp.zeros((256, 128), F32)
        dv = jnp.zeros((256, 128), F32)
        for qi in range(2):
            span = slice(qi * 128, qi * 128 + 640)
            dp = nt(V[hp, span, :], DD[hp, 2 + qi])
            p = E[qi, hp]
            ds = (p.astype(F32) * (dp - C[qi, row, :])).astype(BF16)
            dq = diagonal(nn(KT[hp, :, span], ds)).T * 0.125
            DQ[qi, :, pl.ds(pl.multiple_of(hp * 128, 128), 128)] = dq.astype(BF16)
            own = slice((2 - qi) * 128, (4 - qi) * 128)
            dk = dk + nn(ds[own], QQ[hp, 2 + qi])
            dv = dv + nn(p[own], DD[hp, 2 + qi])
        DK[hp] = dk
        DV[hp] = dv

    def foreign_back(side, final):
        q1, q2, k2 = sides[side]
        c1, c2 = (0, 1) if side == 0 else (1, 0)

        @pl.loop(0, 8)
        def _(hp):
            row = pl.ds(hp, 1)
            p1 = PF[side, hp, 0:256]
            ds1 = (p1.astype(F32) * (nt(V[hp, 256:512, :], DD[hp, q1]) - CR[side, c1, row, :])).astype(BF16)
            dk = DK[hp] + nn(ds1, QQ[hp, q1])
            dv = DV[hp] + nn(p1, DD[hp, q1])
            p2 = PF[side, hp, 256:384]
            ds2 = (p2.astype(F32) * (nt(V[hp, k2 : k2 + 128, :], DD[hp, q2]) - CR[side, c2, row, :])).astype(BF16)
            dk2 = nn(ds2, QQ[hp, q2])
            dv2 = nn(p2, DD[hp, q2])
            if side == 0:
                dk = jnp.concatenate([dk[:128] + dk2, dk[128:]], axis=0)
                dv = jnp.concatenate([dv[:128] + dv2, dv[128:]], axis=0)
            else:
                dk = jnp.concatenate([dk[:128], dk[128:] + dk2], axis=0)
                dv = jnp.concatenate([dv[:128], dv[128:] + dv2], axis=0)
            if final:
                lanes = pl.ds(pl.multiple_of(hp * 128, 128), 128)
                DKB[:, lanes] = dk.astype(BF16)
                DVB[:, lanes] = dv.astype(BF16)
            else:
                DK[hp] = dk
                DV[hp] = dv

    for c in g_near:
        c.wait_recv()
    d_mix(4, 2, False)
    c_near.wait_recv()
    foreign_back(1, False)

    @pl.loop(0, 4)
    def _(j):
        lanes = pl.ds(pl.multiple_of(j * 256, 256), 256)
        DO[:, lanes] = DO[:, lanes] + nt(DQ[...].reshape(256, 1024), WQ[lanes, :])

    @pl.when(has_far)
    def _():
        for c in g_far:
            c.wait_recv()

    d_mix(0, 2, False)

    @pl.when(has_far)
    def _():
        c_far.wait_recv()

    foreign_back(0, True)

    @pl.loop(0, 4)
    def _(j):
        lanes = pl.ds(pl.multiple_of(j * 256, 256), 256)
        r = (DO[:, lanes] + nt(DKB[...], WK[lanes, :]) + nt(DVB[...], WV[lanes, :])).astype(BF16)
        out_ref[pl.ds(pl.multiple_of(core * 128, 128), 128), lanes] = r[:128]
        out_ref[pl.ds(pl.multiple_of((1 - core) * 128, 128), 128), lanes] = r[128:]

    @pl.loop(1, ng)
    def _(d):
        told(d).wait_recv()

    loss_ref[...] = jnp.sum(LS[...], axis=0)

    @pl.when(has_far)
    def _():
        for c in x_far + g_far + [l_far, c_far]:
            c.wait_send()

    for c in x_near + g_near + [l_near, c_near]:
        c.wait_send()

    @pl.loop(1, ne)
    def _(d):
        a1(d).wait_send()
        a2(d).wait_send()

    @pl.loop(1, ng)
    def _(d):
        tell(d).wait_send()


def shards(x, wq, wk, wv, wo, decoder, targets, area_weight, key_blocks):
    ne, ng = lax.axis_size("ens"), lax.axis_size("grid")
    points, channels = x.shape[1:]
    variables = decoder.shape[0]
    start = lax.axis_index("ens") * (points // ne)
    truth = lax.dynamic_slice_in_dim(targets, start, points // ne, 1).T
    truth = jnp.pad(truth, ((0, 0), (0, 128 - variables)))
    weight = lax.dynamic_slice_in_dim(area_weight, start, points // ne, 0)
    weight = jnp.pad(jnp.broadcast_to(weight[:, None], (points // ne, variables)), ((0, 0), (0, 128 - variables)))
    padded = jnp.pad(decoder, ((0, 128 - variables), (0, 0)))
    vm = pltpu.VMEM
    dma = pltpu.SemaphoreType.DMA
    scratch = [vm((1024, 1024), BF16)] * 4 + [
        vm((128, 1024), BF16),
        vm((6, 128, 1024), BF16),
        vm((8, 768, 128), BF16),
        vm((8, 768, 128), BF16),
        vm((8, 128, 768), BF16),
        vm((8, 128, 768), BF16),
        vm((8, 6, 256, 128), BF16),
        vm((8, 6, 256, 128), BF16),
        vm((2, 8, 640, 256), BF16),
        vm((2, 8, 128, 128), F32),
        vm((2, 3, 8, 256), F32),
        vm((2, 8, 256), F32),
        vm((2, 8, 256), F32),
        vm((2, 3, 8, 256), F32),
        vm((2, 3, 8, 256), F32),
        vm((2, 128, 1024), F32),
        vm((2, 128, 1024), BF16),
        vm((2, 128, 1024), BF16),
        vm((2, 128, 128), BF16),
        vm((16, 16, 128), BF16),
        vm((16, 16, 128), F32),
        vm((16, 16, 128), BF16),
        vm((6, 128, 128), BF16),
        vm((2, 8, 384, 256), BF16),
        vm((256, 1024), F32),
        vm((768, 1024), BF16),
        vm((2, 128, 1024), BF16),
        vm((8, 256, 128), F32),
        vm((8, 256, 128), F32),
        vm((256, 1024), BF16),
        vm((256, 1024), BF16),
        vm((2, 8, 256), F32),
        vm((2, 2, 8, 256), F32),
        vm((16, 8, 128), F32),
        dma((7,)),
        dma((4,)),
        dma((4,)),
        dma((16,)),
        dma((16,)),
        dma((16,)),
        dma((16,)),
        dma((4,)),
        dma((4,)),
        dma((2,)),
        dma((2,)),
        dma((2,)),
        dma((2,)),
        dma((16,)),
        dma((16,)),
    ]
    anywhere = pl.BlockSpec(memory_space=pl.ANY)
    in_vmem = pl.BlockSpec(memory_space=pltpu.VMEM)
    grad, loss = pl.pallas_call(
        functools.partial(kernel, ne, ng),
        out_shape=(
            jax.ShapeDtypeStruct((points, channels), BF16),
            jax.ShapeDtypeStruct((8, 128), F32),
        ),
        in_specs=[pl.BlockSpec(memory_space=pltpu.SMEM)] + [anywhere] * 6 + [in_vmem] * 2,
        out_specs=(in_vmem, in_vmem),
        scratch_shapes=scratch,
        compiler_params=pltpu.CompilerParams(
            collective_id=0, has_side_effects=True, vmem_limit_bytes=58 * 1024 * 1024
        ),
        name="whole",
    )(key_blocks, x[0], wq, wk, wv, wo, padded, truth, weight)
    return grad[None], loss[0, 0] / (points * ng * variables)


def solution(mesh):
    return jax.shard_map(
        shards,
        mesh=mesh,
        in_specs=(
            P("ens", "grid", None),
            P(),
            P(),
            P(),
            P(),
            P(),
            P(None, "grid"),
            P("grid"),
            P("grid", None),
        ),
        out_specs=(P("ens", "grid", None), P()),
        check_vma=False,
    )
```

profile of v0, /device:TPU:4, one launch (start us, length us, event | category | flops | bytes accessed | tf_op | source)
XLA Modules:
  0.0 94.7 jit_solution(16413002198879858705)
XLA Ops:
  0.6 0.0 copy-start
  0.7 0.8 dynamic_slice.7
  1.4 0.1 broadcast_in_dim.4
  1.5 0.6 pad.13.weight_ref
  2.1 0.0 copy-done
  2.1 0.1 constant_dynamic-slice_fusion
  2.2 0.1 copy.12
  2.3 0.6 pad.12.truth_ref
  2.9 1.7 %pad.11.mp_hbm = bf16[128,1024]{1,0:T(8,128)(2,1)} pad(bf16[100,1024]{1,0:T(8,128)(2,1)} %param.14, bf16[]{:T(256)} %constant.11.clone.1), padding=0_28x0_0 | pad | bytes 466946 | tf_op jit(solution)/shard_map/jit(_pad)/pad | solution.py:581
  4.5 85.3 %whole.1 = (bf16[256,1024]{1,0:T(8,128)(2,1)}, f32[8,128]{1,0:T(8,128)}) custom-call(s32[2,3]{1,0:T(2,128)} %kb_ref.1, bf16[256,1024]{1,0:T(8,128)(2,1)} %bitcast.4, bf16[1024,1024]{1,0:T(8,128)(2,1)} %wq_hbm.1, bf16[1024,1024]{1,0:T(8,128)(2,1)} %wk_hbm.1, bf16[1024,1024]{1,0:T(8,128)(2,1)} %wv_hbm.1, bf16[1024,1024]{1,0:T(8,128)(2,1)} %wo_hbm.1, ...), custom_call_target="tpu_custom_call" | custom-call | tf_op jit(solution)/shard_map/whole/pallas_call | solution.py:637
  89.8 1.2 %slice.3 = f32[1,1]{1,0:T(1,128)} slice(f32[8,128]{1,0:T(8,128)} %get-tuple-element.5), slice={[0:1], [0:1]} | slice | bytes 8 | tf_op jit(solution)/shard_map/slice | solution.py:651
  91.7 1.9 %copy.14 = bf16[1,256,1024]{2,1,0:T(8,128)(2,1)} copy(bf16[1,256,1024]{2,1,0:T(8,128)(2,1)} %bitcast.5) | data formatting | bytes 1048576
Async XLA Ops:
  0.6 1.5 %copy-start = (f32[100,256]{1,0:T(8,128)S(1)}, f32[100,256]{1,0:T(8,128)}, u32[]{:S(2)}) copy-start(f32[100,256]{1,0:T(8,128)} %param.15) | copy-start | bytes 307204
where the time goes:
time: 95.5 us; the launch traced here: 94.7 us
  Pallas kernels  85.3 us (89%)
  local copies, waits for them, and re-layouts  6.95 us (7%)
  between operations  2.44 us (3%)
    pallas_call x1, Pallas kernels, shards(): pl.pallas_call(functools.partial(kernel, ne, ng), out_shape=(jax.ShapeDty...  85.3 us
    unnamed x4, local copies, waits for them, and re-layouts  1.94 us

commit v1 on v0

--- a/solution.py
+++ b/solution.py
@@ -13,6 +13,9 @@
 NEG = -1e30
 F32 = jnp.float32
 BF16 = jnp.bfloat16
+UNROLL = 8
+UNROLL_OWN = 2
+UNROLL_BACK = 4
 
 
 def nt(a, b):
@@ -37,18 +40,37 @@
     return jnp.concatenate([pair[:64, :128], pair[64:, 128:]], axis=0)
 
 
+def unrolled(count, group, body):
+    if group == count:
+        for i in range(count):
+            body(i)
+    else:
+
+        @pl.loop(0, count // group)
+        def _(k):
+            for i in range(group):
+                body(k * group + i)
+
+
+def span(i, width):
+    if isinstance(i, int):
+        return slice(i * width, (i + 1) * width)
+    return pl.ds(pl.multiple_of(i * width, width), width)
+
+
 def kernel(
     ne,
     ng,
+    variables,
     kb_ref,
+    area_ref,
     x_hbm,
     wq_hbm,
     wk_hbm,
     wv_hbm,
     wo_hbm,
-    mp_hbm,
-    truth_ref,
-    weight_ref,
+    decoder_ref,
+    targets_ref,
     out_ref,
     loss_ref,
     WQ,
@@ -56,6 +78,8 @@
     WV,
     WO,
     MP,
+    MW,
+    TT,
     X,
     K,
     V,
@@ -72,7 +96,7 @@
     LR,
     MIXF,
     MIXB,
-    OUTB,
+    FX,
     FC,
     RV,
     Y,
@@ -80,7 +104,6 @@
     GF,
     PF,
     DO,
-    DOB,
     DQ,
     DK,
     DV,
@@ -120,8 +143,8 @@
         load(x_hbm.at[pl.ds(pl.multiple_of((1 - core) * 128, 128), 128)], X.at[3], 1),
     ]
     lk, lv, lq = load(wk_hbm, WK, 2), load(wv_hbm, WV, 3), load(wq_hbm, WQ, 4)
-    lo, lm = load(wo_hbm, WO, 5), load(mp_hbm, MP, 6)
-    for c in lx + [lk, lv, lq, lo, lm]:
+    lo = load(wo_hbm, WO, 5)
+    for c in lx + [lk, lv, lq, lo]:
         c.start()
 
     barrier = pltpu.get_barrier_semaphore()
@@ -155,8 +178,7 @@
 
     @pl.when(has_far)
     def _():
-        for c in x_far:
-            c.start()
+        x_far[0].start()
 
     for c in x_near:
         c.start()
@@ -178,30 +200,31 @@
     def rows_of(ref, slot, count):
         return ref[slot : slot + count].reshape(count * 128, 1024)
 
-    def project_kv(W, D, DT, slot, count):
-        @pl.loop(0, 4)
-        def _(j):
-            r = nn(rows_of(X, slot, count), W[:, pl.ds(pl.multiple_of(j * 256, 256), 256)]).astype(BF16)
+    def project_kv(W, D, DT, slot, count, group=1):
+        def tile(j):
+            r = nn(rows_of(X, slot, count), W[:, span(j, 256)]).astype(BF16)
             for h in range(2):
                 part = r[:, h * 128 : (h + 1) * 128]
                 D[2 * j + h, slot * 128 : (slot + count) * 128, :] = part
                 DT[2 * j + h, :, slot * 128 : (slot + count) * 128] = part.T
 
-    def project_q(slot, count):
-        @pl.loop(0, 4)
-        def _(j):
-            r = nn(rows_of(X, slot, count), WQ[:, pl.ds(pl.multiple_of(j * 256, 256), 256)]).astype(BF16)
+        unrolled(4, group, tile)
+
+    def project_q(slot, count, group=1):
+        def tile(j):
+            r = nn(rows_of(X, slot, count), WQ[:, span(j, 256)]).astype(BF16)
             r = (r.astype(F32) * 0.125).astype(BF16)
             for h in range(2):
                 for i in range(count):
                     QQ[2 * j + h, slot + i] = stacked(r[i * 128 : (i + 1) * 128, h * 128 : (h + 1) * 128])
 
-    def attend(qi, first, last, step, final):
+        unrolled(4, group, tile)
+
+    def attend(qi, first, last, step, final, group=1):
         n = last - first + 1
         off = (first - qi) * 128
 
-        @pl.loop(0, 8)
-        def _(hp):
+        def head_pair(hp):
             row = pl.ds(hp, 1)
             s = nt(K[hp, first * 128 : (last + 1) * 128, :], QQ[hp, 2 + qi])
             if step:
@@ -229,21 +252,18 @@
             if final:
                 LSE[qi, row, :] = m + jnp.log(total)
                 mix = (acc * heads_of(1.0 / total)).T
-                lanes = pl.ds(pl.multiple_of(hp * 128, 128), 128)
+                lanes = span(hp, 128)
                 MIXF[qi, :, lanes] = mix
                 MIXB[qi, :, lanes] = mix.astype(BF16)
             else:
                 L[qi, row, :] = total
                 ACC[qi, hp] = acc
 
+        unrolled(8, group, head_pair)
+
     def decode(qi):
-        @pl.loop(0, 4)
-        def _(j):
-            lanes = pl.ds(pl.multiple_of(j * 256, 256), 256)
-            r = X[2 + qi, :, lanes].astype(F32) + nn(MIXB[qi], WO[:, lanes])
-            OUTB[qi, :, lanes] = r.astype(BF16)
-
-        FC[qi] = nt(OUTB[qi], MP[...]).astype(BF16)
+        f = nt(MIXB[qi], MW[...])
+        FC[qi] = (FX[qi] + (f[:, :128] + f[:, 128:])).astype(BF16)
 
     def place(t):
         half = t // 8
@@ -265,28 +285,45 @@
     project_kv(WK, K, KT, 4, 2)
     project_kv(WV, V, VT, 4, 2)
     attend(0, 2, 4, 0, False)
+
+    @pl.when(has_far)
+    def _():
+        x_far[0].wait_send()
+        x_far[1].start()
+
     attend(1, 2, 5, 0, False)
     project_q(4, 2)
+    MP[...] = jnp.concatenate([decoder_ref[...], jnp.zeros((28, 1024), BF16)], axis=0)
+    TT[...] = jnp.concatenate([targets_ref[...], jnp.zeros((28, 256), F32)], axis=0).T
     lo.wait()
-    lm.wait()
+
+    @pl.loop(0, 4)
+    def _(j):
+        r = nt(MP[...], WO[span(j, 256), :])
+        hi = r.astype(BF16)
+        MW[0:128, span(j, 256)] = hi
+        MW[128:256, span(j, 256)] = (r - hi.astype(F32)).astype(BF16)
+
+    for qi in range(2):
+        FX[qi] = nt(X[2 + qi], MP[...])
 
     @pl.when(has_far)
     def _():
         x_far[0].wait_recv()
 
-    project_kv(WK, K, KT, 1, 1)
-    project_kv(WV, V, VT, 1, 1)
-    attend(1, 1, 1, 1, True)
-    attend(0, 1, 1, 1, False)
+    project_kv(WK, K, KT, 1, 1, 4)
+    project_kv(WV, V, VT, 1, 1, 4)
+    attend(1, 1, 1, 1, True, UNROLL)
+    attend(0, 1, 1, 1, False, UNROLL)
     decode(1)
 
     @pl.when(has_far)
     def _():
         x_far[1].wait_recv()
 
-    project_kv(WK, K, KT, 0, 1)
-    project_kv(WV, V, VT, 0, 1)
-    attend(0, 0, 0, 2, True)
+    project_kv(WK, K, KT, 0, 1, 4)
+    project_kv(WV, V, VT, 0, 1, 4)
+    attend(0, 0, 0, 2, True, UNROLL)
     decode(0)
 
     @pl.loop(1, ne)
@@ -345,8 +382,12 @@
         a1(d).wait_recv()
 
     Y[...] = RV[...].astype(F32)
-    truth = truth_ref[...]
-    weight = weight_ref[...]
+    truth = TT[pl.ds(pl.multiple_of(e * 16, 16), 16), :]
+    line = lax.broadcasted_iota(jnp.int32, (16, 128), 0)
+    weight = jnp.zeros((16, 128), F32)
+    for i in range(16):
+        weight = jnp.where(line == i, area_ref[e * 16 + i], weight)
+    weight = jnp.where(lax.broadcasted_iota(jnp.int32, (16, 128), 1) < variables, weight, 0.0)
 
     def score(i, total):
         y = Y[i]
@@ -429,33 +470,27 @@
     def _(d):
         tell(d).start()
 
-    indicator = (lax.broadcasted_iota(jnp.int32, (8, 128), 1) // 64) == lax.broadcasted_iota(jnp.int32, (8, 128), 0)
-    indicator = jnp.where(indicator, 1.0, 0.0).astype(BF16)
+    pair_of = lax.broadcasted_iota(jnp.int32, (16, 1024), 0)
+    pair_of = 2 * lax.rem(pair_of, 8) + pair_of // 8
+    indicator = jnp.where(lax.broadcasted_iota(jnp.int32, (16, 1024), 1) // 64 == pair_of, 1.0, 0.0).astype(BF16)
 
     def d_mix(slot, count, own):
-        @pl.loop(0, 4)
-        def _(j):
-            lanes = pl.ds(pl.multiple_of(j * 256, 256), 256)
-            r = nn(GF[slot : slot + count].reshape(count * 128, 128), MP[:, lanes])
-            if own:
-                DO[:, lanes] = r
-            DOB[slot * 128 : (slot + count) * 128, lanes] = r.astype(BF16)
-
-        @pl.loop(0, 4)
-        def _(j):
-            lanes = pl.ds(pl.multiple_of(j * 256, 256), 256)
-            r = nt(DOB[slot * 128 : (slot + count) * 128, :], WO[lanes, :]).astype(BF16)
+        rows = GF[slot : slot + count].reshape(count * 128, 128)
+        twice = jnp.concatenate([rows, rows], axis=1)
+        c = jnp.zeros((16, 256), F32)
+        for j in range(4):
+            r = nn(twice, MW[:, span(j, 256)]).astype(BF16)
             for h in range(2):
                 for i in range(count):
-                    part = r[i * 128 : (i + 1) * 128, h * 128 : (h + 1) * 128]
-                    DD[2 * j + h, slot + i] = stacked(part)
-                    if own:
-                        hp_lanes = pl.ds(pl.multiple_of(j * 256 + h * 128, 128), 128)
-                        prod = part.astype(F32) * MIXF[i, :, hp_lanes]
-                        hi = prod.astype(BF16)
-                        low_part = (prod - hi.astype(F32)).astype(BF16)
-                        c = nt(indicator, hi) + nt(indicator, low_part)
-                        C[i, pl.ds(2 * j + h, 1), :] = jnp.concatenate([c[0:1], c[1:2]], axis=1)
+                    DD[2 * j + h, slot + i] = stacked(r[i * 128 : (i + 1) * 128, h * 128 : (h + 1) * 128])
+            if own:
+                prod = r.astype(F32) * MIXF[:, :, span(j, 256)].reshape(256, 256)
+                hi = prod.astype(BF16)
+                lower = (prod - hi.astype(F32)).astype(BF16)
+                c = c + nt(indicator[:, span(j, 256)], hi) + nt(indicator[:, span(j, 256)], lower)
+        if own:
+            for i in range(2):
+                C[i] = jnp.concatenate([c[0:8, span(i, 128)], c[8:16, span(i, 128)]], axis=1)
 
     d_mix(2, 2, True)
     c_far = to(C, CR.at[0], cs.at[0], cr.at[0], (e, far))
@@ -467,30 +502,30 @@
 
     c_near.start()
 
-    @pl.loop(0, 8)
-    def _(hp):
+    def own_back(hp):
         row = pl.ds(hp, 1)
         dk = jnp.zeros((256, 128), F32)
         dv = jnp.zeros((256, 128), F32)
         for qi in range(2):
-            span = slice(qi * 128, qi * 128 + 640)
-            dp = nt(V[hp, span, :], DD[hp, 2 + qi])
+            window = slice(qi * 128, qi * 128 + 640)
+            dp = nt(V[hp, window, :], DD[hp, 2 + qi])
             p = E[qi, hp]
             ds = (p.astype(F32) * (dp - C[qi, row, :])).astype(BF16)
-            dq = diagonal(nn(KT[hp, :, span], ds)).T * 0.125
-            DQ[qi, :, pl.ds(pl.multiple_of(hp * 128, 128), 128)] = dq.astype(BF16)
+            dq = diagonal(nn(KT[hp, :, window], ds)).T * 0.125
+            DQ[qi, :, span(hp, 128)] = dq.astype(BF16)
             own = slice((2 - qi) * 128, (4 - qi) * 128)
             dk = dk + nn(ds[own], QQ[hp, 2 + qi])
             dv = dv + nn(p[own], DD[hp, 2 + qi])
         DK[hp] = dk
         DV[hp] = dv
 
+    unrolled(8, UNROLL_OWN, own_back)
+
     def foreign_back(side, final):
         q1, q2, k2 = sides[side]
         c1, c2 = (0, 1) if side == 0 else (1, 0)
 
-        @pl.loop(0, 8)
-        def _(hp):
+        def head_pair(hp):
             row = pl.ds(hp, 1)
             p1 = PF[side, hp, 0:256]
             ds1 = (p1.astype(F32) * (nt(V[hp, 256:512, :], DD[hp, q1]) - CR[side, c1, row, :])).astype(BF16)
@@ -507,23 +542,25 @@
                 dk = jnp.concatenate([dk[:128], dk[128:] + dk2], axis=0)
                 dv = jnp.concatenate([dv[:128], dv[128:] + dv2], axis=0)
             if final:
-                lanes = pl.ds(pl.multiple_of(hp * 128, 128), 128)
+                lanes = span(hp, 128)
                 DKB[:, lanes] = dk.astype(BF16)
                 DVB[:, lanes] = dv.astype(BF16)
             else:
                 DK[hp] = dk
                 DV[hp] = dv
 
+        unrolled(8, UNROLL_BACK, head_pair)
+
     for c in g_near:
         c.wait_recv()
     d_mix(4, 2, False)
     c_near.wait_recv()
     foreign_back(1, False)
 
-    @pl.loop(0, 4)
-    def _(j):
-        lanes = pl.ds(pl.multiple_of(j * 256, 256), 256)
-        DO[:, lanes] = DO[:, lanes] + nt(DQ[...].reshape(256, 1024), WQ[lanes, :])
+    for j in range(4):
+        lanes = span(j, 256)
+        own_rows = GF[2:4].reshape(256, 128)
+        DO[:, lanes] = nn(own_rows, MP[:, lanes]) + nt(DQ[...].reshape(256, 1024), WQ[lanes, :])
 
     @pl.when(has_far)
     def _():
@@ -538,9 +575,8 @@
 
     foreign_back(0, True)
 
-    @pl.loop(0, 4)
-    def _(j):
-        lanes = pl.ds(pl.multiple_of(j * 256, 256), 256)
+    for j in range(4):
+        lanes = span(j, 256)
         r = (DO[:, lanes] + nt(DKB[...], WK[lanes, :]) + nt(DVB[...], WV[lanes, :])).astype(BF16)
         out_ref[pl.ds(pl.multiple_of(core * 128, 128), 128), lanes] = r[:128]
         out_ref[pl.ds(pl.multiple_of((1 - core) * 128, 128), 128), lanes] = r[128:]
@@ -549,11 +585,11 @@
     def _(d):
         told(d).wait_recv()
 
-    loss_ref[...] = jnp.sum(LS[...], axis=0)
-
-    @pl.when(has_far)
-    def _():
-        for c in x_far + g_far + [l_far, c_far]:
+    loss_ref[...] = jnp.sum(LS[...], axis=0)[0:1, 0:1] * (1.0 / (256 * ng * variables))
+
+    @pl.when(has_far)
+    def _():
+        for c in [x_far[1]] + g_far + [l_far, c_far]:
             c.wait_send()
 
     for c in x_near + g_near + [l_near, c_near]:
@@ -573,16 +609,12 @@
     ne, ng = lax.axis_size("ens"), lax.axis_size("grid")
     points, channels = x.shape[1:]
     variables = decoder.shape[0]
-    start = lax.axis_index("ens") * (points // ne)
-    truth = lax.dynamic_slice_in_dim(targets, start, points // ne, 1).T
-    truth = jnp.pad(truth, ((0, 0), (0, 128 - variables)))
-    weight = lax.dynamic_slice_in_dim(area_weight, start, points // ne, 0)
-    weight = jnp.pad(jnp.broadcast_to(weight[:, None], (points // ne, variables)), ((0, 0), (0, 128 - variables)))
-    padded = jnp.pad(decoder, ((0, 128 - variables), (0, 0)))
     vm = pltpu.VMEM
     dma = pltpu.SemaphoreType.DMA
     scratch = [vm((1024, 1024), BF16)] * 4 + [
         vm((128, 1024), BF16),
+        vm((256, 1024), BF16),
+        vm((256, 128), F32),
         vm((6, 128, 1024), BF16),
         vm((8, 768, 128), BF16),
         vm((8, 768, 128), BF16),
@@ -599,7 +631,7 @@
         vm((2, 3, 8, 256), F32),
         vm((2, 128, 1024), F32),
         vm((2, 128, 1024), BF16),
-        vm((2, 128, 1024), BF16),
+        vm((2, 128, 128), F32),
         vm((2, 128, 128), BF16),
         vm((16, 16, 128), BF16),
         vm((16, 16, 128), F32),
@@ -607,7 +639,6 @@
         vm((6, 128, 128), BF16),
         vm((2, 8, 384, 256), BF16),
         vm((256, 1024), F32),
-        vm((768, 1024), BF16),
         vm((2, 128, 1024), BF16),
         vm((8, 256, 128), F32),
         vm((8, 256, 128), F32),
@@ -635,20 +666,20 @@
     anywhere = pl.BlockSpec(memory_space=pl.ANY)
     in_vmem = pl.BlockSpec(memory_space=pltpu.VMEM)
     grad, loss = pl.pallas_call(
-        functools.partial(kernel, ne, ng),
+        functools.partial(kernel, ne, ng, variables),
         out_shape=(
             jax.ShapeDtypeStruct((points, channels), BF16),
-            jax.ShapeDtypeStruct((8, 128), F32),
+            jax.ShapeDtypeStruct((1, 1), F32),
         ),
-        in_specs=[pl.BlockSpec(memory_space=pltpu.SMEM)] + [anywhere] * 6 + [in_vmem] * 2,
+        in_specs=[pl.BlockSpec(memory_space=pltpu.SMEM)] * 2 + [anywhere] * 5 + [in_vmem] * 2,
         out_specs=(in_vmem, in_vmem),
         scratch_shapes=scratch,
         compiler_params=pltpu.CompilerParams(
             collective_id=0, has_side_effects=True, vmem_limit_bytes=58 * 1024 * 1024
         ),
         name="whole",
-    )(key_blocks, x[0], wq, wk, wv, wo, padded, truth, weight)
-    return grad[None], loss[0, 0] / (points * ng * variables)
+    )(key_blocks, area_weight, x[0], wq, wk, wv, wo, decoder, targets)
+    return grad[None], loss[0, 0]
 
 
 def solution(mesh):

time: 95.5 us -> 74.6 us (0.78)
  Pallas kernels: 85.3 us -> 70.2 us
  local copies, waits for them, and re-layouts: 6.95 us -> 1.87 us
    pallas_call x1, Pallas kernels: 85.3 us -> 70.2 us  [shards(): pl.pallas_call(functools.partial(kernel, ne, ng, variables), out_shape=(j...]
    pad x3 -> x0, local copies, waits for them, and re-layouts: 2.87 us -> none  [the longest x1 1.66 us: shards(): padded = jnp.pad(decoder, ((0, 128 - variables), (0, 0)))]
    slice x1 -> x0, local copies, waits for them, and re-layouts: 1.2 us -> none  [shards(): return (grad[None], loss[0, 0] / (points * ng * variables))]
    unnamed x4 -> x1, local copies, waits for them, and re-layouts: 1.94 us -> 1.87 us
where the time goes in v1:
time: 74.6 us; the launch traced here: 74.4 us
  Pallas kernels  70.2 us (94%)
  between operations  2.34 us (3%)
  local copies, waits for them, and re-layouts  1.87 us (3%)
    pallas_call x1, Pallas kernels, shards(): pl.pallas_call(functools.partial(kernel, ne, ng, variables), out_shape=(j...  70.2 us
    unnamed x1, local copies, waits for them, and re-layouts  1.87 us

profile of v1, /device:TPU:4, one launch (start us, length us, event | category | flops | bytes accessed | tf_op | source)
XLA Modules:
  0.0 74.4 jit_solution(6037377952879362549)
XLA Ops:
  0.6 70.2 %whole.1 = (bf16[256,1024]{1,0:T(8,128)(2,1)}, f32[1,1]{1,0:T(1,128)}) custom-call(s32[2,3]{1,0:T(2,128)} %kb_ref.1, f32[256]{0:T(256)} %area_ref.1, bf16[256,1024]{1,0:T(8,128)(2,1)} %bitcast.3, bf16[1024,1024]{1,0:T(8,128)(2,1)} %wq_hbm.1, bf16[1024,1024]{1,0:T(8,128)(2,1)} %wk_hbm.1, bf16[1024,1024]{1,0:T(8,128)(2,1)} %wv_hbm.1, ...), custom_call_target="tpu_custom_call" | custom-call | tf_op jit(solution)/shard_map/whole/pallas_call | solution.py:668
  70.9 1.9 %copy.13 = bf16[1,256,1024]{2,1,0:T(8,128)(2,1)} copy(bf16[1,256,1024]{2,1,0:T(8,128)(2,1)} %bitcast.4) | data formatting | bytes 1048576

commit v2 on v1

--- a/solution.py
+++ b/solution.py
@@ -14,8 +14,8 @@
 F32 = jnp.float32
 BF16 = jnp.bfloat16
 UNROLL = 8
-UNROLL_OWN = 2
-UNROLL_BACK = 4
+UNROLL_OWN = 8
+UNROLL_BACK = 8
 
 
 def nt(a, b):
@@ -92,8 +92,16 @@
     MS,
     L,
     LSE,
+    SO,
+    SR,
+    LB,
+    PS,
+    PR,
+    MXF,
     LO,
     LR,
+    LF,
+    LFR,
     MIXF,
     MIXB,
     FX,
@@ -123,6 +131,8 @@
     gr,
     ls,
     lr,
+    ps,
+    pr,
     cs,
     cr,
     ts,
@@ -161,7 +171,11 @@
     def _():
         X[0:2] = jnp.zeros((2, 128, 1024), BF16)
         GF[0:2] = jnp.zeros((2, 128, 128), BF16)
-        LR[0] = jnp.full((3, 8, 256), BIG, F32)
+        LFR[...] = jnp.full((8, 256), BIG, F32)
+        SR[0] = jnp.zeros((8, 256), F32)
+        SR[1] = jnp.ones((8, 256), F32)
+        SR[2:4] = jnp.full((2, 8, 256), BIG, F32)
+        PR[...] = jnp.zeros((128, 128), BF16)
         CR[0] = jnp.zeros((2, 8, 256), F32)
 
     for c in lx:
@@ -186,9 +200,10 @@
     def slot_of(block):
         return jnp.where(core == 0, block - (2 * g - 2), 2 * g + 3 - block)
 
-    seen = []
+    seen, picked = [], []
     for q in range(2):
         ids = [jnp.where(core == 0, slot_of(kb_ref[q, n]), slot_of(kb_ref[1 - q, n])) for n in range(3)]
+        picked.append([jnp.clip(i, q, q + 4) for i in ids])
         seen.append([(ids[0] == s) | (ids[1] == s) | (ids[2] == s) for s in range(6)])
 
     low = lax.broadcasted_iota(jnp.int32, (1, 128), 1) < 64
@@ -200,13 +215,19 @@
     def rows_of(ref, slot, count):
         return ref[slot : slot + count].reshape(count * 128, 1024)
 
-    def project_kv(W, D, DT, slot, count, group=1):
+    def project_kv(slot, count, group=1):
         def tile(j):
-            r = nn(rows_of(X, slot, count), W[:, span(j, 256)]).astype(BF16)
+            rows = slice(slot * 128, (slot + count) * 128)
+            k = nn(rows_of(X, slot, count), WK[:, span(j, 256)]).astype(BF16)
+            v = nn(rows_of(X, slot, count), WV[:, span(j, 256)]).astype(BF16)
             for h in range(2):
-                part = r[:, h * 128 : (h + 1) * 128]
-                D[2 * j + h, slot * 128 : (slot + count) * 128, :] = part
-                DT[2 * j + h, :, slot * 128 : (slot + count) * 128] = part.T
+                part = k[:, span(h, 128)]
+                K[2 * j + h, rows, :] = part
+                for i in range(count):
+                    KT[2 * j + h, slot + i] = part[span(i, 128)].T
+                part = v[:, span(h, 128)]
+                V[2 * j + h, slot : slot + count] = part.reshape(count, 128, 128)
+                VT[2 * j + h, :, rows] = part.T
 
         unrolled(4, group, tile)
 
@@ -222,7 +243,7 @@
 
     def attend(qi, first, last, step, final, group=1):
         n = last - first + 1
-        off = (first - qi) * 128
+        off = first - qi
 
         def head_pair(hp):
             row = pl.ds(hp, 1)
@@ -242,7 +263,7 @@
                 total = total + jnp.sum(x, axis=0, keepdims=True)
                 exps.append(x.astype(BF16))
             eb = jnp.concatenate(exps, axis=0) if n > 1 else exps[0]
-            E[qi, hp, off : off + n * 128, :] = eb
+            E[qi, hp, off : off + n] = eb.reshape(n, 128, 256)
             acc = diagonal(nn(VT[hp, :, first * 128 : (last + 1) * 128], eb))
             if step:
                 alpha = jnp.exp(m_old - m)
@@ -276,20 +297,22 @@
 
     lk.wait()
     lv.wait()
-    project_kv(WK, K, KT, 2, 2)
-    project_kv(WV, V, VT, 2, 2)
+    project_kv(2, 2)
     lq.wait()
     project_q(2, 2)
     for c in x_near:
         c.wait_recv()
-    project_kv(WK, K, KT, 4, 2)
-    project_kv(WV, V, VT, 4, 2)
+    project_kv(4, 2)
     attend(0, 2, 4, 0, False)
-
-    @pl.when(has_far)
-    def _():
-        x_far[0].wait_send()
-        x_far[1].start()
+    SO[0] = MS[0, 0]
+    SO[1] = L[0]
+    SO[2] = jnp.full((8, 256), jnp.where(seen[0][1], 0.0, BIG), F32)
+    SO[3] = jnp.full((8, 256), jnp.where(seen[0][0], 0.0, BIG), F32)
+    s_far = to(SO, SR, ps.at[0], pr.at[0], (e, far))
+
+    @pl.when(has_far)
+    def _():
+        s_far.start()
 
     attend(1, 2, 5, 0, False)
     project_q(4, 2)
@@ -309,26 +332,86 @@
 
     @pl.when(has_far)
     def _():
+        x_far[0].wait_send()
+        x_far[1].start()
         x_far[0].wait_recv()
-
-    project_kv(WK, K, KT, 1, 1, 4)
-    project_kv(WV, V, VT, 1, 1, 4)
+        s_far.wait_recv()
+
+    def far_query(hp):
+        row = pl.ds(hp, 1)
+        s = nt(K[hp, 256:512, :], QQ[hp, 1])
+        m_old, bias_a, bias_b = SR[0, row, :], SR[2, row, :], SR[3, row, :]
+        m = jnp.maximum(m_old, jnp.max(s[:128], axis=0, keepdims=True) - bias_a)
+        m = jnp.maximum(m, jnp.max(s[128:], axis=0, keepdims=True) - bias_b)
+        xa, xb = jnp.exp(s[:128] - (m + bias_a)), jnp.exp(s[128:] - (m + bias_b))
+        total = SR[1, row, :] * jnp.exp(m_old - m)
+        total = total + jnp.sum(xa, axis=0, keepdims=True) + jnp.sum(xb, axis=0, keepdims=True)
+        LB[0, row, :] = m + jnp.log(total)
+        p = (jnp.concatenate([xa, xb], axis=0) * (1.0 / total)).astype(BF16)
+        PF[0, hp, 0:256] = p
+        MXF[:, span(hp, 128)] = diagonal(nn(VT[hp, :, 256:512], p)).T.astype(BF16)
+
+    project_q(1, 1, 4)
+    unrolled(8, UNROLL, far_query)
+    f = nt(MXF[...], MW[...])
+    PS[...] = (f[:, :128] + f[:, 128:]).astype(BF16)
+    p_far = [to(PS, PR, ps.at[1], pr.at[1], (e, far)), to(LB.at[0], LB.at[1], ps.at[2], pr.at[2], (e, far))]
+
+    @pl.when(has_far)
+    def _():
+        for c in p_far:
+            c.start()
+
+    @pl.when(jnp.logical_not(has_far))
+    def _():
+        LB[1] = MS[0, 0] + jnp.log(L[0])
+
+    project_kv(1, 1, 4)
     attend(1, 1, 1, 1, True, UNROLL)
-    attend(0, 1, 1, 1, False, UNROLL)
     decode(1)
 
-    @pl.when(has_far)
-    def _():
-        x_far[1].wait_recv()
-
-    project_kv(WK, K, KT, 0, 1, 4)
-    project_kv(WV, V, VT, 0, 1, 4)
-    attend(0, 0, 0, 2, True, UNROLL)
-    decode(0)
-
-    @pl.loop(1, ne)
-    def _(d):
-        a1(d).start()
+    def a1_half(near_block):
+        half = jnp.where(near_block, 1 - core, core)
+
+        @pl.loop(0, 8)
+        def _(i):
+            t = half * 8 + i
+
+            @pl.when(t != e)
+            def _():
+                a1(lax.rem(t - e + ne, ne)).start()
+
+    a1_half(True)
+
+    def normalise(qi, hp, spans):
+        row = pl.ds(hp, 1)
+        lse = LSE[qi, row, :]
+        for step, (first, last) in enumerate(spans):
+            scale = jnp.exp(MS[qi, step, row, :] - lse)
+            a, b = first - qi, last + 1 - qi
+            E[qi, hp, a:b] = (E[qi, hp, a:b].astype(F32) * scale).astype(BF16)
+
+    @pl.loop(0, 8)
+    def _(hp):
+        normalise(1, hp, ((2, 5), (1, 1)))
+
+    @pl.when(has_far)
+    def _():
+        for c in p_far:
+            c.wait_recv()
+
+    LSE[0] = LB[1]
+
+    def far_block(hp):
+        row = pl.ds(hp, 1)
+        mix = (ACC[0, hp] * heads_of(jnp.exp(MS[0, 0, row, :] - LSE[0, row, :]))).T
+        MIXF[0, :, span(hp, 128)] = mix
+        MIXB[0, :, span(hp, 128)] = mix.astype(BF16)
+
+    unrolled(8, 8, far_block)
+    f = nt(MIXB[0], MW[...])
+    FC[0] = (FX[0] + (f[:, :128] + f[:, 128:]) + PR[...].astype(F32)).astype(BF16)
+    a1_half(False)
 
     b_own, r_own = place(e)
     RV[e] = FC[b_own, pl.ds(r_own, 16), :]
@@ -336,46 +419,56 @@
     def shown(qi, s):
         return jnp.where(seen[qi][s], LSE[qi], BIG)
 
-    LO[0, 0], LO[0, 1], LO[0, 2] = shown(0, 1), shown(0, 0), shown(1, 1)
-    LO[1, 0], LO[1, 1], LO[1, 2] = shown(1, 5), shown(1, 4), shown(0, 4)
-    l_far = to(LO.at[0], LR.at[0], ls.at[0], lr.at[0], (e, far))
-    l_near = to(LO.at[1], LR.at[1], ls.at[1], lr.at[1], (e, near))
+    LF[...] = shown(1, 1)
+    LO[0], LO[1], LO[2] = shown(1, 5), shown(1, 4), shown(0, 4)
+    l_far = to(LF, LFR, ls.at[0], lr.at[0], (e, far))
+    l_near = to(LO, LR, ls.at[1], lr.at[1], (e, near))
 
     @pl.when(has_far)
     def _():
         l_far.start()
 
     l_near.start()
+
+    @pl.loop(0, 8)
+    def _(hp):
+        normalise(0, hp, ((2, 4),))
+
+    l_near.wait_recv()
 
     @pl.loop(0, 8)
     def _(hp):
         row = pl.ds(hp, 1)
-        for qi in range(2):
-            lse = LSE[qi, row, :]
-            spans = ((2, 4), (1, 1), (0, 0)) if qi == 0 else ((2, 5), (1, 1))
-            for step, (first, last) in enumerate(spans):
-                scale = jnp.exp(MS[qi, step, row, :] - lse)
-                a, b = (first - qi) * 128, (last + 1 - qi) * 128
-                E[qi, hp, a:b, :] = (E[qi, hp, a:b, :].astype(F32) * scale).astype(BF16)
-
-    project_q(0, 2)
-
-    sides = ((1, 0, 256), (4, 5, 384))
-
-    def foreign(side):
-        q1, q2, k2 = sides[side]
+        s1 = nt(K[hp, 256:512, :], QQ[hp, 4])
+        PF[1, hp, 0:128] = jnp.exp(s1[:128] - LR[0, row, :]).astype(BF16)
+        PF[1, hp, 128:256] = jnp.exp(s1[128:] - LR[1, row, :]).astype(BF16)
+        s2 = nt(K[hp, 384:512, :], QQ[hp, 5])
+        PF[1, hp, 256:384] = jnp.exp(s2 - LR[2, row, :]).astype(BF16)
+
+    def second_far():
+        @pl.when(has_far)
+        def _():
+            x_far[1].wait_recv()
+            l_far.wait_recv()
+
+        project_kv(0, 1)
+        project_q(0, 1)
 
         @pl.loop(0, 8)
         def _(hp):
             row = pl.ds(hp, 1)
-            s1 = nt(K[hp, 256:512, :], QQ[hp, q1])
-            PF[side, hp, 0:128] = jnp.exp(s1[:128] - LR[side, 0, row, :]).astype(BF16)
-            PF[side, hp, 128:256] = jnp.exp(s1[128:] - LR[side, 1, row, :]).astype(BF16)
-            s2 = nt(K[hp, k2 : k2 + 128, :], QQ[hp, q2])
-            PF[side, hp, 256:384] = jnp.exp(s2 - LR[side, 2, row, :]).astype(BF16)
-
-    l_near.wait_recv()
-    foreign(1)
+            lse = LSE[0, row, :]
+            s = nt(K[hp, 0:256, :], QQ[hp, 2])
+            pa = jnp.exp(s[:128] - jnp.where(seen[0][0], lse, BIG))
+            pb = jnp.exp(s[128:] - jnp.where(seen[0][1], lse, BIG))
+            p = jnp.concatenate([pa, pb], axis=0).astype(BF16)
+            E[0, hp, 0:2] = p.reshape(2, 128, 256)
+            lanes = span(hp, 128)
+            MIXF[0, :, lanes] = MIXF[0, :, lanes] + diagonal(nn(VT[hp, :, 0:256], p)).T
+            s2 = nt(K[hp, 256:384, :], QQ[hp, 0])
+            PF[0, hp, 256:384] = jnp.exp(s2 - LFR[row, :]).astype(BF16)
+
+    sides = ((1, 0, 2), (4, 5, 3))
 
     @pl.loop(1, ne)
     def _(d):
@@ -428,11 +521,7 @@
 
     GF[2 + b_own, pl.ds(r_own, 16), :] = G[e]
 
-    @pl.when(has_far)
-    def _():
-        l_far.wait_recv()
-
-    foreign(0)
+    second_far()
 
     def a2_in(d):
         b, r = place(lax.rem(e - d + ne, ne))
@@ -504,20 +593,25 @@
 
     def own_back(hp):
         row = pl.ds(hp, 1)
-        dk = jnp.zeros((256, 128), F32)
-        dv = jnp.zeros((256, 128), F32)
+        dks, dvs = [], []
         for qi in range(2):
-            window = slice(qi * 128, qi * 128 + 640)
-            dp = nt(V[hp, window, :], DD[hp, 2 + qi])
-            p = E[qi, hp]
-            ds = (p.astype(F32) * (dp - C[qi, row, :])).astype(BF16)
-            dq = diagonal(nn(KT[hp, :, window], ds)).T * 0.125
+            other = [jnp.where(i == 3 - qi, 1.0, 0.0) for i in picked[qi][1:]]
+            dp = nt(jnp.concatenate([V[hp, i] for i in picked[qi]], axis=0), DD[hp, 2 + qi])
+            p = [E[qi, hp, i - qi].astype(F32) for i in picked[qi]]
+            c = C[qi, row, :]
+            ds = [p[n] * (dp[n * 128 : (n + 1) * 128] - c) for n in range(3)]
+            half = [x.astype(BF16) for x in ds]
+            keys = jnp.concatenate([KT[hp, i] for i in picked[qi]], axis=1)
+            dq = diagonal(nn(keys, jnp.concatenate(half, axis=0))).T * 0.125
             DQ[qi, :, span(hp, 128)] = dq.astype(BF16)
-            own = slice((2 - qi) * 128, (4 - qi) * 128)
-            dk = dk + nn(ds[own], QQ[hp, 2 + qi])
-            dv = dv + nn(p[own], DD[hp, 2 + qi])
-        DK[hp] = dk
-        DV[hp] = dv
+            pair = [half[0], (ds[1] * other[0] + ds[2] * other[1]).astype(BF16)]
+            prob = [E[qi, hp, 2], (p[1] * other[0] + p[2] * other[1]).astype(BF16)]
+            if qi:
+                pair, prob = pair[::-1], prob[::-1]
+            dks.append(nn(jnp.concatenate(pair, axis=0), QQ[hp, 2 + qi]))
+            dvs.append(nn(jnp.concatenate(prob, axis=0), DD[hp, 2 + qi]))
+        DK[hp] = dks[0] + dks[1]
+        DV[hp] = dvs[0] + dvs[1]
 
     unrolled(8, UNROLL_OWN, own_back)
 
@@ -528,11 +622,11 @@
         def head_pair(hp):
             row = pl.ds(hp, 1)
             p1 = PF[side, hp, 0:256]
-            ds1 = (p1.astype(F32) * (nt(V[hp, 256:512, :], DD[hp, q1]) - CR[side, c1, row, :])).astype(BF16)
+            ds1 = (p1.astype(F32) * (nt(V[hp, 2:4].reshape(256, 128), DD[hp, q1]) - CR[side, c1, row, :])).astype(BF16)
             dk = DK[hp] + nn(ds1, QQ[hp, q1])
             dv = DV[hp] + nn(p1, DD[hp, q1])
             p2 = PF[side, hp, 256:384]
-            ds2 = (p2.astype(F32) * (nt(V[hp, k2 : k2 + 128, :], DD[hp, q2]) - CR[side, c2, row, :])).astype(BF16)
+            ds2 = (p2.astype(F32) * (nt(V[hp, k2], DD[hp, q2]) - CR[side, c2, row, :])).astype(BF16)
             dk2 = nn(ds2, QQ[hp, q2])
             dv2 = nn(p2, DD[hp, q2])
             if side == 0:
@@ -589,7 +683,7 @@
 
     @pl.when(has_far)
     def _():
-        for c in [x_far[1]] + g_far + [l_far, c_far]:
+        for c in [x_far[1], s_far] + p_far + g_far + [l_far, c_far]:
             c.wait_send()
 
     for c in x_near + g_near + [l_near, c_near]:
@@ -617,18 +711,26 @@
         vm((256, 128), F32),
         vm((6, 128, 1024), BF16),
         vm((8, 768, 128), BF16),
-        vm((8, 768, 128), BF16),
-        vm((8, 128, 768), BF16),
+        vm((8, 6, 128, 128), BF16),
+        vm((8, 6, 128, 128), BF16),
         vm((8, 128, 768), BF16),
         vm((8, 6, 256, 128), BF16),
         vm((8, 6, 256, 128), BF16),
-        vm((2, 8, 640, 256), BF16),
+        vm((2, 8, 5, 128, 256), BF16),
         vm((2, 8, 128, 128), F32),
         vm((2, 3, 8, 256), F32),
         vm((2, 8, 256), F32),
         vm((2, 8, 256), F32),
-        vm((2, 3, 8, 256), F32),
-        vm((2, 3, 8, 256), F32),
+        vm((4, 8, 256), F32),
+        vm((4, 8, 256), F32),
+        vm((2, 8, 256), F32),
+        vm((128, 128), BF16),
+        vm((128, 128), BF16),
+        vm((128, 1024), BF16),
+        vm((3, 8, 256), F32),
+        vm((3, 8, 256), F32),
+        vm((8, 256), F32),
+        vm((8, 256), F32),
         vm((2, 128, 1024), F32),
         vm((2, 128, 1024), BF16),
         vm((2, 128, 128), F32),
@@ -658,6 +760,8 @@
         dma((4,)),
         dma((2,)),
         dma((2,)),
+        dma((3,)),
+        dma((3,)),
         dma((2,)),
         dma((2,)),
         dma((16,)),

time: 74.6 us -> 77.9 us (1.044)
  Pallas kernels: 70.2 us -> 73 us
    pallas_call x1, Pallas kernels: 70.2 us -> 73 us  [shards(): pl.pallas_call(functools.partial(kernel, ne, ng, variables), out_shape=(j...]
where the time goes in v2:
time: 77.9 us; the launch traced here: 77.2 us
  Pallas kernels  73 us (94%)
  between operations  2.34 us (3%)
  local copies, waits for them, and re-layouts  1.87 us (2%)
    pallas_call x1, Pallas kernels, shards(): pl.pallas_call(functools.partial(kernel, ne, ng, variables), out_shape=(j...  73 us
    unnamed x1, local copies, waits for them, and re-layouts  1.87 us

profile of v2, /device:TPU:4, one launch (start us, length us, event | category | flops | bytes accessed | tf_op | source)
XLA Modules:
  0.0 77.2 jit_solution(5486180847487338742)
XLA Ops:
  0.6 73.0 %whole.1 = (bf16[256,1024]{1,0:T(8,128)(2,1)}, f32[1,1]{1,0:T(1,128)}) custom-call(s32[2,3]{1,0:T(2,128)} %kb_ref.1, f32[256]{0:T(256)} %area_ref.1, bf16[256,1024]{1,0:T(8,128)(2,1)} %bitcast.3, bf16[1024,1024]{1,0:T(8,128)(2,1)} %wq_hbm.1, bf16[1024,1024]{1,0:T(8,128)(2,1)} %wk_hbm.1, bf16[1024,1024]{1,0:T(8,128)(2,1)} %wv_hbm.1, ...), custom_call_target="tpu_custom_call" | custom-call | tf_op jit(solution)/shard_map/whole/pallas_call | solution.py:772
  73.7 1.9 %copy.13 = bf16[1,256,1024]{2,1,0:T(8,128)(2,1)} copy(bf16[1,256,1024]{2,1,0:T(8,128)(2,1)} %bitcast.4) | data formatting | bytes 1048576

commit v3 on v2

--- a/solution.py
+++ b/solution.py
@@ -215,7 +215,7 @@
     def rows_of(ref, slot, count):
         return ref[slot : slot + count].reshape(count * 128, 1024)
 
-    def project_kv(slot, count, group=1):
+    def project_kv(slot, count, group=4):
         def tile(j):
             rows = slice(slot * 128, (slot + count) * 128)
             k = nn(rows_of(X, slot, count), WK[:, span(j, 256)]).astype(BF16)
@@ -231,17 +231,16 @@
 
         unrolled(4, group, tile)
 
-    def project_q(slot, count, group=1):
+    def project_q(slot, count, group=4):
         def tile(j):
-            r = nn(rows_of(X, slot, count), WQ[:, span(j, 256)]).astype(BF16)
-            r = (r.astype(F32) * 0.125).astype(BF16)
+            r = (nn(rows_of(X, slot, count), WQ[:, span(j, 256)]) * 0.125).astype(BF16)
             for h in range(2):
                 for i in range(count):
                     QQ[2 * j + h, slot + i] = stacked(r[i * 128 : (i + 1) * 128, h * 128 : (h + 1) * 128])
 
         unrolled(4, group, tile)
 
-    def attend(qi, first, last, step, final, group=1):
+    def attend(qi, first, last, step, final, group=8):
         n = last - first + 1
         off = first - qi
 
@@ -320,8 +319,7 @@
     TT[...] = jnp.concatenate([targets_ref[...], jnp.zeros((28, 256), F32)], axis=0).T
     lo.wait()
 
-    @pl.loop(0, 4)
-    def _(j):
+    for j in range(4):
         r = nt(MP[...], WO[span(j, 256), :])
         hi = r.astype(BF16)
         MW[0:128, span(j, 256)] = hi
@@ -391,9 +389,7 @@
             a, b = first - qi, last + 1 - qi
             E[qi, hp, a:b] = (E[qi, hp, a:b].astype(F32) * scale).astype(BF16)
 
-    @pl.loop(0, 8)
-    def _(hp):
-        normalise(1, hp, ((2, 5), (1, 1)))
+    unrolled(8, 4, lambda hp: normalise(1, hp, ((2, 5), (1, 1))))
 
     @pl.when(has_far)
     def _():
@@ -430,14 +426,11 @@
 
     l_near.start()
 
-    @pl.loop(0, 8)
-    def _(hp):
-        normalise(0, hp, ((2, 4),))
+    unrolled(8, 4, lambda hp: normalise(0, hp, ((2, 4),)))
 
     l_near.wait_recv()
 
-    @pl.loop(0, 8)
-    def _(hp):
+    def near_query(hp):
         row = pl.ds(hp, 1)
         s1 = nt(K[hp, 256:512, :], QQ[hp, 4])
         PF[1, hp, 0:128] = jnp.exp(s1[:128] - LR[0, row, :]).astype(BF16)
@@ -445,6 +438,8 @@
         s2 = nt(K[hp, 384:512, :], QQ[hp, 5])
         PF[1, hp, 256:384] = jnp.exp(s2 - LR[2, row, :]).astype(BF16)
 
+    unrolled(8, 8, near_query)
+
     def second_far():
         @pl.when(has_far)
         def _():
@@ -454,8 +449,7 @@
         project_kv(0, 1)
         project_q(0, 1)
 
-        @pl.loop(0, 8)
-        def _(hp):
+        def head_pair(hp):
             row = pl.ds(hp, 1)
             lse = LSE[0, row, :]
             s = nt(K[hp, 0:256, :], QQ[hp, 2])
@@ -467,6 +461,8 @@
             MIXF[0, :, lanes] = MIXF[0, :, lanes] + diagonal(nn(VT[hp, :, 0:256], p)).T
             s2 = nt(K[hp, 256:384, :], QQ[hp, 0])
             PF[0, hp, 256:384] = jnp.exp(s2 - LFR[row, :]).astype(BF16)
+
+        unrolled(8, 8, head_pair)
 
     sides = ((1, 0, 2), (4, 5, 3))
 
@@ -772,7 +768,7 @@
     grad, loss = pl.pallas_call(
         functools.partial(kernel, ne, ng, variables),
         out_shape=(
-            jax.ShapeDtypeStruct((points, channels), BF16),
+            pltpu.VMEM((points, channels), BF16),
             jax.ShapeDtypeStruct((1, 1), F32),
         ),
         in_specs=[pl.BlockSpec(memory_space=pltpu.SMEM)] * 2 + [anywhere] * 5 + [in_vmem] * 2,

time: 77.9 us -> 70.5 us (0.905)
  Pallas kernels: 73 us -> 66.1 us
  local copies, waits for them, and re-layouts: 1.87 us -> 0.8 us
    pallas_call x1, Pallas kernels: 73 us -> 66.1 us  [shards(): pl.pallas_call(functools.partial(kernel, ne, ng, variables), out_shape=(p...]
    unnamed x1, local copies, waits for them, and re-layouts: 1.87 us -> 0.8 us
where the time goes in v3:
time: 70.5 us; the launch traced here: 69.2 us
  Pallas kernels  66.1 us (94%)
  between operations  2.33 us (3%)
  local copies, waits for them, and re-layouts  0.8 us (1%)
    pallas_call x1, Pallas kernels, shards(): pl.pallas_call(functools.partial(kernel, ne, ng, variables), out_shape=(p...  66.1 us

profile of v3, /device:TPU:4, one launch (start us, length us, event | category | flops | bytes accessed | tf_op | source)
XLA Modules:
  0.0 69.2 jit_solution(13219352979004363845)
XLA Ops:
  0.6 66.1 %whole.1 = (bf16[256,1024]{1,0:T(8,128)(2,1)S(1)}, f32[1,1]{1,0:T(1,128)}) custom-call(s32[2,3]{1,0:T(2,128)} %kb_ref.1, f32[256]{0:T(256)} %area_ref.1, bf16[256,1024]{1,0:T(8,128)(2,1)} %bitcast.4, bf16[1024,1024]{1,0:T(8,128)(2,1)} %wq_hbm.1, bf16[1024,1024]{1,0:T(8,128)(2,1)} %wk_hbm.1, bf16[1024,1024]{1,0:T(8,128)(2,1)} %wv_hbm.1, ...), custom_call_target="tpu_custom_call" | custom-call | tf_op jit(solution)/shard_map/whole/pallas_call | solution.py:768
  66.7 0.8 %copy.13 = bf16[1,256,1024]{2,1,0:T(8,128)(2,1)} copy(bf16[1,256,1024]{2,1,0:T(8,128)(2,1)S(1)} %bitcast.3) | data formatting | bytes 1048576

commit v4 on v3

--- a/solution.py
+++ b/solution.py
@@ -14,6 +14,7 @@
 F32 = jnp.float32
 BF16 = jnp.bfloat16
 UNROLL = 8
+FIRST, SECOND = 4, 6
 UNROLL_OWN = 8
 UNROLL_BACK = 8
 
@@ -107,7 +108,6 @@
     FX,
     FC,
     RV,
-    Y,
     G,
     GF,
     PF,
@@ -173,8 +173,7 @@
         GF[0:2] = jnp.zeros((2, 128, 128), BF16)
         LFR[...] = jnp.full((8, 256), BIG, F32)
         SR[0] = jnp.zeros((8, 256), F32)
-        SR[1] = jnp.ones((8, 256), F32)
-        SR[2:4] = jnp.full((2, 8, 256), BIG, F32)
+        SR[1] = jnp.full((8, 256), BIG, F32)
         PR[...] = jnp.zeros((128, 128), BF16)
         CR[0] = jnp.zeros((2, 8, 256), F32)
 
@@ -187,12 +186,21 @@
             src_ref=src, dst_ref=dst, send_sem=s, recv_sem=r, device_id=dev, device_id_type=MESH
         )
 
-    x_far = [to(X.at[2], X.at[1], xs.at[0], xr.at[0], (e, far)), to(X.at[3], X.at[0], xs.at[1], xr.at[1], (e, far))]
+    x_far = to(X.at[2], X.at[1], xs.at[0], xr.at[0], (e, far))
+    x_sec = [
+        to(X.at[3, span(i, 16)], X.at[0, span(i, 16)], xs.at[4 + i], xr.at[4 + i], (e, far)) for i in range(8)
+    ]
+
+    def second(first, last):
+        @pl.when(has_far)
+        def _():
+            for c in x_sec[first:last]:
+                c.start()
     x_near = [to(X.at[3], X.at[4], xs.at[2], xr.at[2], (e, near)), to(X.at[2], X.at[5], xs.at[3], xr.at[3], (e, near))]
 
     @pl.when(has_far)
     def _():
-        x_far[0].start()
+        x_far.start()
 
     for c in x_near:
         c.start()
@@ -303,10 +311,9 @@
         c.wait_recv()
     project_kv(4, 2)
     attend(0, 2, 4, 0, False)
-    SO[0] = MS[0, 0]
-    SO[1] = L[0]
-    SO[2] = jnp.full((8, 256), jnp.where(seen[0][1], 0.0, BIG), F32)
-    SO[3] = jnp.full((8, 256), jnp.where(seen[0][0], 0.0, BIG), F32)
+    SO[0] = MS[0, 0] + jnp.log(L[0])
+    SO[1, 0:4] = jnp.full((4, 256), jnp.where(seen[0][1], 0.0, BIG), F32)
+    SO[1, 4:8] = jnp.full((4, 256), jnp.where(seen[0][0], 0.0, BIG), F32)
     s_far = to(SO, SR, ps.at[0], pr.at[0], (e, far))
 
     @pl.when(has_far)
@@ -330,19 +337,20 @@
 
     @pl.when(has_far)
     def _():
-        x_far[0].wait_send()
-        x_far[1].start()
-        x_far[0].wait_recv()
+        x_far.wait_send()
+        for c in x_sec[:FIRST]:
+            c.start()
+        x_far.wait_recv()
         s_far.wait_recv()
 
     def far_query(hp):
         row = pl.ds(hp, 1)
         s = nt(K[hp, 256:512, :], QQ[hp, 1])
-        m_old, bias_a, bias_b = SR[0, row, :], SR[2, row, :], SR[3, row, :]
+        m_old, bias_a, bias_b = SR[0, row, :], SR[1, 0:1, :], SR[1, 4:5, :]
         m = jnp.maximum(m_old, jnp.max(s[:128], axis=0, keepdims=True) - bias_a)
         m = jnp.maximum(m, jnp.max(s[128:], axis=0, keepdims=True) - bias_b)
         xa, xb = jnp.exp(s[:128] - (m + bias_a)), jnp.exp(s[128:] - (m + bias_b))
-        total = SR[1, row, :] * jnp.exp(m_old - m)
+        total = jnp.exp(m_old - m)
         total = total + jnp.sum(xa, axis=0, keepdims=True) + jnp.sum(xb, axis=0, keepdims=True)
         LB[0, row, :] = m + jnp.log(total)
         p = (jnp.concatenate([xa, xb], axis=0) * (1.0 / total)).astype(BF16)
@@ -363,6 +371,8 @@
     @pl.when(jnp.logical_not(has_far))
     def _():
         LB[1] = MS[0, 0] + jnp.log(L[0])
+
+    second(FIRST, SECOND)
 
     project_kv(1, 1, 4)
     attend(1, 1, 1, 1, True, UNROLL)
@@ -425,6 +435,7 @@
         l_far.start()
 
     l_near.start()
+    second(SECOND, 8)
 
     unrolled(8, 4, lambda hp: normalise(0, hp, ((2, 4),)))
 
@@ -443,7 +454,8 @@
     def second_far():
         @pl.when(has_far)
         def _():
-            x_far[1].wait_recv()
+            for c in x_sec:
+                c.wait_recv()
             l_far.wait_recv()
 
         project_kv(0, 1)
@@ -470,41 +482,46 @@
     def _(d):
         a1(d).wait_recv()
 
-    Y[...] = RV[...].astype(F32)
     truth = TT[pl.ds(pl.multiple_of(e * 16, 16), 16), :]
     line = lax.broadcasted_iota(jnp.int32, (16, 128), 0)
+    lane = lax.broadcasted_iota(jnp.int32, (16, 128), 1)
     weight = jnp.zeros((16, 128), F32)
     for i in range(16):
         weight = jnp.where(line == i, area_ref[e * 16 + i], weight)
-    weight = jnp.where(lax.broadcasted_iota(jnp.int32, (16, 128), 1) < variables, weight, 0.0)
-
-    def score(i, total):
-        y = Y[i]
-        d = y - truth
-        v = d * d + SMOOTH * SMOOTH
-        r = lax.rsqrt(v)
-        pd = y[None] - Y[...]
-        pv = pd * pd + SMOOTH * SMOOTH
-        pr = lax.rsqrt(pv)
-        grad = weight * (d * r - jnp.sum(pd * pr, axis=0) / (ne - 1))
-        G[i] = grad.astype(BF16)
-        return total + (v * r - jnp.sum(pv * pr, axis=0) / (2.0 * (ne - 1)))
-
-    total = lax.fori_loop(0, ne, score, jnp.zeros((16, 128), F32))
-    partial = jnp.sum(jnp.sum(total * weight, axis=0, keepdims=True), axis=1, keepdims=True)
+    weight = jnp.where(lane < variables, weight, 0.0)
+    members = [RV[i].astype(F32) for i in range(ne)]
+    halves, total = [], jnp.zeros((8, 128), F32)
+    for half in (slice(0, 8), slice(8, 16)):
+        y = [x[half] for x in members]
+        pulls = [jnp.zeros((8, 128), F32) for _ in range(ne)]
+        pairs = jnp.zeros((8, 128), F32)
+        for i in range(ne):
+            for j in range(i + 1, ne):
+                d = y[i] - y[j]
+                v = d * d + SMOOTH * SMOOTH
+                r = lax.rsqrt(v)
+                u = d * r
+                pulls[i] = pulls[i] + u
+                pulls[j] = pulls[j] - u
+                pairs = pairs + v * r
+        score = (2.0 * pairs + ne * SMOOTH) * (-0.5 / (ne - 1))
+        grads = []
+        for i in range(ne):
+            d = y[i] - truth[half]
+            v = d * d + SMOOTH * SMOOTH
+            r = lax.rsqrt(v)
+            score = score + v * r
+            grads.append(weight[half] * (d * r - pulls[i] * (1.0 / (ne - 1))))
+        total = total + weight[half] * score
+        halves.append(grads)
+    partial = jnp.sum(jnp.sum(total, axis=0, keepdims=True), axis=1, keepdims=True)
     p_hi = partial.astype(BF16).astype(F32)
     p_mid = (partial - p_hi).astype(BF16).astype(F32)
     p_lo = partial - p_hi - p_mid
-    lane = lax.broadcasted_iota(jnp.int32, (16, 128), 1)
-    first_row = lax.broadcasted_iota(jnp.int32, (16, 128), 0) == 0
     rider = jnp.where(lane == 104, p_hi, jnp.where(lane == 105, p_mid, jnp.where(lane == 106, p_lo, 0.0)))
-    rider = jnp.where(first_row, rider, 0.0)
-
-    def ride(i, carry):
-        G[i] = (G[i].astype(F32) + rider).astype(BF16)
-        return carry
-
-    lax.fori_loop(0, ne, ride, 0)
+    rider = jnp.where(line == 0, rider, 0.0)
+    for i in range(ne):
+        G[i] = (jnp.concatenate([halves[0][i], halves[1][i]], axis=0) + rider).astype(BF16)
 
     def a2(d):
         t = lax.rem(e + d, ne)
@@ -679,7 +696,7 @@
 
     @pl.when(has_far)
     def _():
-        for c in [x_far[1], s_far] + p_far + g_far + [l_far, c_far]:
+        for c in x_sec + [s_far] + p_far + g_far + [l_far, c_far]:
             c.wait_send()
 
     for c in x_near + g_near + [l_near, c_near]:
@@ -717,8 +734,8 @@
         vm((2, 3, 8, 256), F32),
         vm((2, 8, 256), F32),
         vm((2, 8, 256), F32),
-        vm((4, 8, 256), F32),
-        vm((4, 8, 256), F32),
+        vm((2, 8, 256), F32),
+        vm((2, 8, 256), F32),
         vm((2, 8, 256), F32),
         vm((128, 128), BF16),
         vm((128, 128), BF16),
@@ -732,7 +749,6 @@
         vm((2, 128, 128), F32),
         vm((2, 128, 128), BF16),
         vm((16, 16, 128), BF16),
-        vm((16, 16, 128), F32),
         vm((16, 16, 128), BF16),
         vm((6, 128, 128), BF16),
         vm((2, 8, 384, 256), BF16),
@@ -746,8 +762,8 @@
         vm((2, 2, 8, 256), F32),
         vm((16, 8, 128), F32),
         dma((7,)),
-        dma((4,)),
-        dma((4,)),
+        dma((12,)),
+        dma((12,)),
         dma((16,)),
         dma((16,)),
         dma((16,)),

time: 70.5 us -> 68 us (0.965); the launches traced: 69.2 us -> 67.5 us
  Pallas kernels: 66.1 us -> 64.3 us
    pallas_call x1, Pallas kernels: 66.1 us -> 64.3 us  [shards(): pl.pallas_call(functools.partial(kernel, ne, ng, variables), out_shape=(p...]
where the time goes in v4:
time: 68 us; the launch traced here: 67.5 us
  Pallas kernels  64.3 us (95%)
  between operations  2.33 us (3%)
  local copies, waits for them, and re-layouts  0.8 us (1%)
    pallas_call x1, Pallas kernels, shards(): pl.pallas_call(functools.partial(kernel, ne, ng, variables), out_shape=(p...  64.3 us

profile of v4, /device:TPU:4, one launch (start us, length us, event | category | flops | bytes accessed | tf_op | source)
XLA Modules:
  0.0 67.5 jit_solution(12118381829015552199)
XLA Ops:
  0.6 64.3 %whole.1 = (bf16[256,1024]{1,0:T(8,128)(2,1)S(1)}, f32[1,1]{1,0:T(1,128)}) custom-call(s32[2,3]{1,0:T(2,128)} %kb_ref.1, f32[256]{0:T(256)} %area_ref.1, bf16[256,1024]{1,0:T(8,128)(2,1)} %bitcast.4, bf16[1024,1024]{1,0:T(8,128)(2,1)} %wq_hbm.1, bf16[1024,1024]{1,0:T(8,128)(2,1)} %wk_hbm.1, bf16[1024,1024]{1,0:T(8,128)(2,1)} %wv_hbm.1, ...), custom_call_target="tpu_custom_call" | custom-call | tf_op jit(solution)/shard_map/whole/pallas_call | solution.py:784
  65.0 0.8 %copy.13 = bf16[1,256,1024]{2,1,0:T(8,128)(2,1)} copy(bf16[1,256,1024]{2,1,0:T(8,128)(2,1)S(1)} %bitcast.3) | data formatting | bytes 1048576

commit v5 on v4

--- a/solution.py
+++ b/solution.py
@@ -359,14 +359,18 @@
 
     project_q(1, 1, 4)
     unrolled(8, UNROLL, far_query)
+    p_far = [to(PS, PR, ps.at[1], pr.at[1], (e, far)), to(LB.at[0], LB.at[1], ps.at[2], pr.at[2], (e, far))]
+
+    @pl.when(has_far)
+    def _():
+        p_far[1].start()
+
     f = nt(MXF[...], MW[...])
     PS[...] = (f[:, :128] + f[:, 128:]).astype(BF16)
-    p_far = [to(PS, PR, ps.at[1], pr.at[1], (e, far)), to(LB.at[0], LB.at[1], ps.at[2], pr.at[2], (e, far))]
-
-    @pl.when(has_far)
-    def _():
-        for c in p_far:
-            c.start()
+
+    @pl.when(has_far)
+    def _():
+        p_far[0].start()
 
     @pl.when(jnp.logical_not(has_far))
     def _():
@@ -555,23 +559,6 @@
     for c in g_near:
         c.start()
 
-    mine = GF[2:4].reshape(256, 128).astype(F32)
-    lane = lax.broadcasted_iota(jnp.int32, (256, 128), 1)
-    mine = jnp.where((lane >= 104) & (lane < 107), mine, 0.0)
-    band = jnp.sum(jnp.sum(mine, axis=0, keepdims=True), axis=1, keepdims=True)
-    LS[g] = jnp.broadcast_to(band, (8, 128))
-
-    def tell(d):
-        return to(LS.at[g], LS.at[g], ts.at[d], tr.at[d], (e, lax.rem(g + d, ng)))
-
-    def told(d):
-        s = lax.rem(g - d + ng, ng)
-        return to(LS.at[s], LS.at[s], ts.at[d], tr.at[d], (e, g))
-
-    @pl.loop(1, ng)
-    def _(d):
-        tell(d).start()
-
     pair_of = lax.broadcasted_iota(jnp.int32, (16, 1024), 0)
     pair_of = 2 * lax.rem(pair_of, 8) + pair_of // 8
     indicator = jnp.where(lax.broadcasted_iota(jnp.int32, (16, 1024), 1) // 64 == pair_of, 1.0, 0.0).astype(BF16)
@@ -603,6 +590,23 @@
         c_far.start()
 
     c_near.start()
+
+    mine = GF[2:4].reshape(256, 128).astype(F32)
+    lane = lax.broadcasted_iota(jnp.int32, (256, 128), 1)
+    mine = jnp.where((lane >= 104) & (lane < 107), mine, 0.0)
+    band = jnp.sum(jnp.sum(mine, axis=0, keepdims=True), axis=1, keepdims=True)
+    LS[g] = jnp.broadcast_to(band, (8, 128))
+
+    def tell(d):
+        return to(LS.at[g], LS.at[g], ts.at[d], tr.at[d], (e, lax.rem(g + d, ng)))
+
+    def told(d):
+        s = lax.rem(g - d + ng, ng)
+        return to(LS.at[s], LS.at[s], ts.at[d], tr.at[d], (e, g))
+
+    @pl.loop(1, ng)
+    def _(d):
+        tell(d).start()
 
     def own_back(hp):
         row = pl.ds(hp, 1)

time: 68 us -> 68 us (level)
  the two profiles are of different devices: /device:TPU:4 before, /device:TPU:6 now
where the time goes in v5:
time: 68 us; the launch traced here: 67.9 us
  Pallas kernels  64.8 us (95%)
  between operations  2.33 us (3%)
  local copies, waits for them, and re-layouts  0.8 us (1%)
    pallas_call x1, Pallas kernels, shards(): pl.pallas_call(functools.partial(kernel, ne, ng, variables), out_shape=(p...  64.8 us

profile of v5, /device:TPU:6, one launch (start us, length us, event | category | flops | bytes accessed | tf_op | source)
XLA Modules:
  0.0 67.9 jit_solution(4474667908380175239)
XLA Ops:
  0.6 64.8 %whole.1 = (bf16[256,1024]{1,0:T(8,128)(2,1)S(1)}, f32[1,1]{1,0:T(1,128)}) custom-call(s32[2,3]{1,0:T(2,128)} %kb_ref.1, f32[256]{0:T(256)} %area_ref.1, bf16[256,1024]{1,0:T(8,128)(2,1)} %bitcast.4, bf16[1024,1024]{1,0:T(8,128)(2,1)} %wq_hbm.1, bf16[1024,1024]{1,0:T(8,128)(2,1)} %wk_hbm.1, bf16[1024,1024]{1,0:T(8,128)(2,1)} %wv_hbm.1, ...), custom_call_target="tpu_custom_call" | custom-call | tf_op jit(solution)/shard_map/whole/pallas_call | solution.py:788
  65.4 0.8 %copy.13 = bf16[1,256,1024]{2,1,0:T(8,128)(2,1)} copy(bf16[1,256,1024]{2,1,0:T(8,128)(2,1)S(1)} %bitcast.3) | data formatting | bytes 1048576
